TPU v7x, 128 devices: a whole 4x4x4 slice. The times are simulated.
128 devices in a mesh: fsdp: 16 (over y_hi, x, core), ctx: 8 (over z, y_lo).
Axes of the slice: x: 4, y: 4 (y_hi: 2, y_lo: 2; y = y_hi * 2 + y_lo), z: 4, core: 2. Of those that a mesh axis runs over, the one named last changes fastest.
Arguments:
- tokens: bfloat16 [16, 2048, 960], P('fsdp', 'ctx'), may hold values from -6 to 6
- attn_gain: bfloat16 [960], P('fsdp'), may hold values from 0.5 to 1.5
- w_query: bfloat16 [960, 960], P('fsdp'), may hold values from -0.1875 to 0.1875
- key_weight: bfloat16 [960, 320], P('fsdp'), may hold values from -0.1875 to 0.1875
- value_weight: bfloat16 [960, 320], P('fsdp'), may hold values from -0.1875 to 0.1875
- w_out: bfloat16 [960, 960], P('fsdp'), may hold values from -0.5 to 0.5
- ffn_gain: bfloat16 [960], P('fsdp'), may hold values from 0.5 to 1.5
- w_gate: bfloat16 [960, 2560], P('fsdp'), may hold values from -0.1875 to 0.1875
- w_up: bfloat16 [960, 2560], P('fsdp'), may hold values from -0.1875 to 0.1875
- w_down: bfloat16 [2560, 960], P('fsdp'), may hold values from -0.125 to 0.125
- d_out: bfloat16 [16, 2048, 960], P('fsdp', 'ctx'), may hold values from -6 to 6
Outputs:
- output: bfloat16 [16, 2048, 960], P('fsdp', 'ctx')
- d_tokens: bfloat16 [16, 2048, 960], P('fsdp', 'ctx')
- grad_attn_gain: float32 [960], P('fsdp')
- grad_query: float32 [960, 960], P('fsdp')
- grad_key: float32 [960, 320], P('fsdp')
- grad_value: float32 [960, 320], P('fsdp')
- grad_out: float32 [960, 960], P('fsdp')
- grad_ffn_gain: float32 [960], P('fsdp')
- grad_gate: float32 [960, 2560], P('fsdp')
- grad_up: float32 [960, 2560], P('fsdp')
- grad_down: float32 [2560, 960], P('fsdp')
All inputs are finite; a program needn't handle non-finite values.
Results may differ from a plain program's by a relative error of at most 0.025.
Values may be sent and summed in bfloat16 or wider, within the bound.
A program may use at most 192 MiB of HBM per device.

v0:
```python
import math

import jax
import jax.numpy as jnp
from jax import lax
from jax.sharding import PartitionSpec as P

QUERY_HEADS = 15
KEY_VALUE_HEADS = 5
HEAD_WIDTH = 64


EPS = 1e-05
ROPE_BASE = 10000.0


def side_by_side(arrays, axis, dim, along):
    widths = [math.prod(a.shape[along:]) for a in arrays]
    both = jnp.concatenate(
        [a.reshape(*a.shape[:along], w) for a, w in zip(arrays, widths)], axis=along
    )
    out = lax.all_gather(both, axis, axis=dim, tiled=True)
    blocks = jnp.split(out, [sum(widths[:k]) for k in range(1, len(widths))], axis=along)
    return tuple((b.reshape(*out.shape[:along], *a.shape[along:]) for a, b in zip(arrays, blocks)))


def sent_together(arrays, axis, dim, along):
    widths = [a.shape[along] for a in arrays]
    both = jnp.concatenate(arrays, axis=along)
    out = lax.all_gather(both, axis, axis=dim, tiled=True)
    return tuple(jnp.split(out, [sum(widths[:k]) for k in range(1, len(widths))], axis=along))


def side_by_side_2(arrays, axis, dim, along):
    ends, at = ([], 0)
    for a in arrays[:-1]:
        at += a.shape[along]
        ends.append(at)
    both = jnp.concatenate(arrays, axis=along)
    return tuple(
        jnp.split(lax.psum_scatter(both, axis, scatter_dimension=dim, tiled=True), ends, axis=along)
    )


def packed_total(arrays, axis):
    line, at, done = (jnp.concatenate([a.reshape(-1) for a in arrays]), 0, [])
    running = lax.psum(line, axis)
    for a in arrays:
        done.append(running[at : at + a.size].reshape(a.shape))
        at += a.size
    return tuple(done)


def tables(token_positions, head_size):
    half = head_size // 2
    freqs = ROPE_BASE ** (-jnp.arange(half, dtype=jnp.float32) * 2.0 / head_size)
    angles = token_positions.astype(jnp.float32)[:, None] * freqs[None, :]
    return (jnp.cos(angles)[None, :, None, :], jnp.sin(angles)[None, :, None, :])


def apply_rotary(value_rows, cosine_table, sine_table):
    half = value_rows.shape[-1] // 2
    first = value_rows[..., :half]
    second = value_rows[..., half:]
    return jnp.concatenate(
        [first * cosine_table - second * sine_table, second * cosine_table + first * sine_table],
        axis=-1,
    )


def inverse_rotary(grads, cosine_table, sine_table):
    half = grads.shape[-1] // 2
    first = grads[..., :half]
    second = grads[..., half:]
    return jnp.concatenate(
        [first * cosine_table + second * sine_table, second * cosine_table - first * sine_table],
        axis=-1,
    )


def norm_scale(value_rows):
    return lax.rsqrt(jnp.mean(value_rows * value_rows, axis=-1, keepdims=True) + EPS)


def norm_back(grad_normed, value_rows, scale, gain):
    unit = value_rows * scale
    grad_gain = jnp.sum(grad_normed * unit, axis=0)
    grad_unit = grad_normed * gain
    grad_values = scale * (grad_unit - unit * jnp.mean(grad_unit * unit, axis=-1, keepdims=True))
    return (grad_values, grad_gain)


def linear_projection(left, right):
    return jnp.dot(left, right, preferred_element_type=jnp.float32)


def project_left(left, right):
    return lax.dot_general(
        left, right, (((0,), (0,)), ((), ())), preferred_element_type=jnp.float32
    )


def project_right(left, right):
    return lax.dot_general(
        left, right, (((1,), (1,)), ((), ())), preferred_element_type=jnp.float32
    )


def head_scores(query_head, keys_head, token_positions):
    sequence_length = keys_head.shape[1]
    scores = jnp.einsum("slge,sme->sglm", query_head, keys_head, preferred_element_type=jnp.float32)
    scores = scores * query_head.shape[-1] ** (-0.5)
    causal = token_positions[:, None] >= jnp.arange(sequence_length, dtype=jnp.int32)[None, :]
    return jnp.where(causal, scores, -1e30)


def on_device(
    tokens,
    attn_gain,
    w_query,
    key_weight,
    value_weight,
    w_out,
    ffn_gain,
    w_gate,
    w_up,
    w_down,
    d_out,
):
    sequence_count, attention_block, width = tokens.shape
    token_count = sequence_count * attention_block
    query_group = QUERY_HEADS // KEY_VALUE_HEADS
    sequence_length = attention_block * lax.axis_size("ctx")
    token_positions = lax.axis_index("ctx") * attention_block + jnp.arange(
        attention_block, dtype=jnp.int32
    )
    cosine_table, sine_table = tables(token_positions, HEAD_WIDTH)
    factor = HEAD_WIDTH ** (-0.5)
    gain_one, query_w, key_matrix, value_matrix, out_w = side_by_side(
        (attn_gain, w_query, key_weight, value_weight, w_out), "fsdp", 0, 1
    )
    flat = tokens.astype(jnp.float32).reshape(token_count, width)
    scale_one = norm_scale(flat)
    normalized_input = (flat * scale_one * gain_one.astype(jnp.float32)).astype(jnp.bfloat16)
    query_rows = linear_projection(normalized_input, query_w).reshape(
        sequence_count, attention_block, QUERY_HEADS, HEAD_WIDTH
    )
    key_rows = linear_projection(normalized_input, key_matrix).reshape(
        sequence_count, attention_block, KEY_VALUE_HEADS, HEAD_WIDTH
    )
    value_rows = (
        linear_projection(normalized_input, value_matrix)
        .astype(jnp.bfloat16)
        .reshape(sequence_count, attention_block, KEY_VALUE_HEADS * HEAD_WIDTH)
    )
    query_r = (
        apply_rotary(query_rows, cosine_table, sine_table)
        .astype(jnp.bfloat16)
        .reshape(sequence_count, attention_block, KEY_VALUE_HEADS, query_group, HEAD_WIDTH)
    )
    key_rows_rotated = (
        apply_rotary(key_rows, cosine_table, sine_table)
        .astype(jnp.bfloat16)
        .reshape(sequence_count, attention_block, KEY_VALUE_HEADS * HEAD_WIDTH)
    )
    key_rows_total, value_rows_total = sent_together((key_rows_rotated, value_rows), "ctx", 1, 0)
    query_heads = jnp.moveaxis(query_r, 2, 0)
    key_rows_per_head = jnp.moveaxis(
        key_rows_total.reshape(sequence_count, sequence_length, KEY_VALUE_HEADS, HEAD_WIDTH), 2, 0
    )
    value_rows_per_head = jnp.moveaxis(
        value_rows_total.reshape(sequence_count, sequence_length, KEY_VALUE_HEADS, HEAD_WIDTH), 2, 0
    )

    def head_forward(operands):
        query_head, keys_head, values_head = operands
        scores = head_scores(query_head, keys_head, token_positions)
        peak = jnp.max(scores, axis=-1, keepdims=True)
        logsum = peak + jnp.log(jnp.sum(jnp.exp(scores - peak), axis=-1, keepdims=True))
        probs_low = jnp.exp(scores - logsum).astype(jnp.bfloat16)
        mixed_head = jnp.einsum(
            "sglm,sme->slge", probs_low, values_head, preferred_element_type=jnp.float32
        )
        return (mixed_head.astype(jnp.bfloat16), logsum)

    mixed_heads, logsums = lax.map(
        head_forward, (query_heads, key_rows_per_head, value_rows_per_head)
    )
    mixed = jnp.moveaxis(mixed_heads, 0, 2).reshape(token_count, QUERY_HEADS * HEAD_WIDTH)
    resid = flat + linear_projection(mixed, out_w)
    gain_two, gate_w, up_w, down_w = (
        *side_by_side((ffn_gain, w_gate, w_up), "fsdp", 0, 1),
        lax.all_gather(w_down, "fsdp", axis=0, tiled=True),
    )
    scale_two = norm_scale(resid)
    normed_two = (resid * scale_two * gain_two.astype(jnp.float32)).astype(jnp.bfloat16)
    gate = linear_projection(normed_two, gate_w)
    up_part = linear_projection(normed_two, up_w)
    sigmoid_gate = jax.nn.sigmoid(gate)
    swish = gate * sigmoid_gate
    hidden = (swish * up_part).astype(jnp.bfloat16)
    output = (resid + linear_projection(hidden, down_w)).astype(jnp.bfloat16).reshape(tokens.shape)
    grad_flat = d_out.reshape(token_count, width)
    grad_down = project_left(hidden, grad_flat)
    grad_hidden = project_right(grad_flat, down_w)
    grad_gate_v = (
        grad_hidden * up_part * sigmoid_gate * (1.0 + gate * (1.0 - sigmoid_gate))
    ).astype(jnp.bfloat16)
    grad_up_v = (grad_hidden * swish).astype(jnp.bfloat16)
    grad_gate = project_left(normed_two, grad_gate_v)
    grad_up = project_left(normed_two, grad_up_v)
    grad_normed_two = project_right(grad_gate_v, gate_w) + project_right(grad_up_v, up_w)
    resid_term, grad_ffn_gain = norm_back(
        grad_normed_two, resid, scale_two, gain_two.astype(jnp.float32)
    )
    grad_resid = grad_flat.astype(jnp.float32) + resid_term
    grad_branch = grad_resid.astype(jnp.bfloat16)
    grad_out = project_left(mixed, grad_branch)
    grad_mixed = (
        project_right(grad_branch, out_w)
        .astype(jnp.bfloat16)
        .reshape(sequence_count, attention_block, KEY_VALUE_HEADS, query_group, HEAD_WIDTH)
    )
    grad_mixed_heads = jnp.moveaxis(grad_mixed, 2, 0)

    def head_backward(operands):
        query_head, keys_head, values_head, grad_head, logsum = operands
        scores = head_scores(query_head, keys_head, token_positions)
        probs = jnp.exp(scores - logsum)
        probs_low = probs.astype(jnp.bfloat16)
        grad_probs = jnp.einsum(
            "slge,sme->sglm", grad_head, values_head, preferred_element_type=jnp.float32
        )
        grad_values_head = jnp.einsum(
            "sglm,slge->sme", probs_low, grad_head, preferred_element_type=jnp.float32
        )
        grad_scores = probs * (grad_probs - jnp.sum(probs * grad_probs, axis=-1, keepdims=True))
        grad_scores = grad_scores.astype(jnp.bfloat16)
        grad_query_head = (
            jnp.einsum("sglm,sme->slge", grad_scores, keys_head, preferred_element_type=jnp.float32)
            * factor
        )
        grad_keys_head = (
            jnp.einsum(
                "sglm,slge->sme", grad_scores, query_head, preferred_element_type=jnp.float32
            )
            * factor
        )
        return (grad_query_head, grad_keys_head, grad_values_head)

    grad_query_heads, gradient_keys_per_head, gradient_values_per_head = lax.map(
        head_backward,
        (query_heads, key_rows_per_head, value_rows_per_head, grad_mixed_heads, logsums),
    )
    grad_query_r = jnp.moveaxis(grad_query_heads, 0, 2)
    gradient_keys_total = jnp.moveaxis(gradient_keys_per_head, 0, 2).reshape(
        sequence_count, sequence_length, KEY_VALUE_HEADS * HEAD_WIDTH
    )
    gradient_values_total = jnp.moveaxis(gradient_values_per_head, 0, 2).reshape(
        sequence_count, sequence_length, KEY_VALUE_HEADS * HEAD_WIDTH
    )
    gradient_keys_local, gradient_values_local = tuple(
        (
            part.astype(jnp.float32)
            for part in side_by_side_2(
                (
                    gradient_keys_total.astype(jnp.bfloat16),
                    gradient_values_total.astype(jnp.bfloat16),
                ),
                "ctx",
                1,
                0,
            )
        )
    )
    grad_query_v = (
        inverse_rotary(
            grad_query_r.reshape(sequence_count, attention_block, QUERY_HEADS, HEAD_WIDTH),
            cosine_table,
            sine_table,
        )
        .astype(jnp.bfloat16)
        .reshape(token_count, QUERY_HEADS * HEAD_WIDTH)
    )
    grad_keys_v = (
        inverse_rotary(
            gradient_keys_local.reshape(
                sequence_count, attention_block, KEY_VALUE_HEADS, HEAD_WIDTH
            ),
            cosine_table,
            sine_table,
        )
        .astype(jnp.bfloat16)
        .reshape(token_count, KEY_VALUE_HEADS * HEAD_WIDTH)
    )
    gradient_values_vector = gradient_values_local.astype(jnp.bfloat16).reshape(
        token_count, KEY_VALUE_HEADS * HEAD_WIDTH
    )
    grad_query = project_left(normalized_input, grad_query_v)
    grad_key = project_left(normalized_input, grad_keys_v)
    grad_value = project_left(normalized_input, gradient_values_vector)
    grad_normed = (
        project_right(grad_query_v, query_w)
        + project_right(grad_keys_v, key_matrix)
        + project_right(gradient_values_vector, value_matrix)
    )
    token_term, grad_attn_gain = norm_back(
        grad_normed, flat, scale_one, gain_one.astype(jnp.float32)
    )
    d_tokens = (grad_resid + token_term).astype(jnp.bfloat16).reshape(tokens.shape)
    (
        part_gain_one,
        part_query,
        part_key,
        part_value,
        part_out,
        part_gain_two,
        part_gate,
        part_up,
        part_down,
    ) = (
        lax.psum_scatter(
            grad_attn_gain.astype(jnp.bfloat16), "fsdp", scatter_dimension=0, tiled=True
        ).astype(jnp.float32),
        lax.psum_scatter(
            grad_query.astype(jnp.bfloat16), "fsdp", scatter_dimension=0, tiled=True
        ).astype(jnp.float32),
        lax.psum_scatter(
            grad_key.astype(jnp.bfloat16), "fsdp", scatter_dimension=0, tiled=True
        ).astype(jnp.float32),
        lax.psum_scatter(
            grad_value.astype(jnp.bfloat16), "fsdp", scatter_dimension=0, tiled=True
        ).astype(jnp.float32),
        lax.psum_scatter(
            grad_out.astype(jnp.bfloat16), "fsdp", scatter_dimension=0, tiled=True
        ).astype(jnp.float32),
        lax.psum_scatter(
            grad_ffn_gain.astype(jnp.bfloat16), "fsdp", scatter_dimension=0, tiled=True
        ).astype(jnp.float32),
        lax.psum_scatter(
            grad_gate.astype(jnp.bfloat16), "fsdp", scatter_dimension=0, tiled=True
        ).astype(jnp.float32),
        lax.psum_scatter(
            grad_up.astype(jnp.bfloat16), "fsdp", scatter_dimension=0, tiled=True
        ).astype(jnp.float32),
        lax.psum_scatter(
            grad_down.astype(jnp.bfloat16), "fsdp", scatter_dimension=0, tiled=True
        ).astype(jnp.float32),
    )
    (
        total_gain_one,
        total_query,
        total_key,
        total_value,
        total_out,
        total_gain_two,
        total_gate,
        total_up,
        total_down,
    ) = tuple(
        (
            part.astype(jnp.float32)
            for part in packed_total(
                (
                    part_gain_one.astype(jnp.bfloat16),
                    part_query.astype(jnp.bfloat16),
                    part_key.astype(jnp.bfloat16),
                    part_value.astype(jnp.bfloat16),
                    part_out.astype(jnp.bfloat16),
                    part_gain_two.astype(jnp.bfloat16),
                    part_gate.astype(jnp.bfloat16),
                    part_up.astype(jnp.bfloat16),
                    part_down.astype(jnp.bfloat16),
                ),
                "ctx",
            )
        )
    )
    return (
        output,
        d_tokens,
        total_gain_one,
        total_query,
        total_key,
        total_value,
        total_out,
        total_gain_two,
        total_gate,
        total_up,
        total_down,
    )


def solution(mesh):
    return jax.shard_map(
        on_device,
        mesh=mesh,
        in_specs=(
            P("fsdp", "ctx", None),
            P("fsdp"),
            P("fsdp", None),
            P("fsdp", None),
            P("fsdp", None),
            P("fsdp", None),
            P("fsdp"),
            P("fsdp", None),
            P("fsdp", None),
            P("fsdp", None),
            P("fsdp", "ctx", None),
        ),
        out_specs=(
            P("fsdp", "ctx", None),
            P("fsdp", "ctx", None),
            P("fsdp"),
            P("fsdp", None),
            P("fsdp", None),
            P("fsdp", None),
            P("fsdp", None),
            P("fsdp"),
            P("fsdp", None),
            P("fsdp", None),
            P("fsdp", None),
        ),
        check_vma=False,
    )
```

profile of v0, /device:TPU:0, one launch (start us, length us, event | category | flops | bytes accessed | tf_op | source)
XLA Modules:
  0.0 734.9 jit_solution(14239708595824433053)
XLA Ops:
  8.0 2.0 concatenate.60
  12.3 62.1 %all-gather.11.cloned.1.call-done = bf16[16,60,2561]{2,1,0:T(8,128)(2,1)} async-done(((bf16[1,60,2561]{2,1,0:T(8,128)(2,1)}), bf16[16,60,2561]{2,1,0:T(8,128)(2,1)}) %all-gather.11.cloned.1.call-update) | async-done | bytes 4917136 | tf_op jit(solution)/shard_map/all_gather | solution.py:22
  74.4 8.0 %reshape.609 = bf16[960,2561]{1,0:T(8,128)(2,1)} reshape(bf16[16,60,2561]{2,1,0:T(8,128)(2,1)} %all-gather.11.cloned.1.call-done) | data formatting | bytes 9834240
  82.4 1.6 slice_bitcast_fusion.1
  85.9 2.4 fusion.107
  90.8 44.8 %all-gather.9.cloned.1.call-done = bf16[2560,960]{1,0:T(8,128)(2,1)} async-done(((bf16[160,960]{1,0:T(8,128)(2,1)}), bf16[2560,960]{1,0:T(8,128)(2,1)}) %all-gather.9.cloned.1.call-update) | async-done | bytes 4915216 | tf_op jit(solution)/shard_map/all_gather | solution.py:193
  135.6 5.5 fusion.124
  141.1 2.5 slice_bitcast_fusion
  143.6 2.8 copy.56
  146.4 2.3 convolution_bitcast_fusion.1
  148.9 47.6 %all-gather.7.cloned.1.call-done = bf16[2,2048,320]{1,2,0:T(8,128)(2,1)} async-done(((bf16[2,256,320]{1,2,0:T(8,128)(2,1)}), bf16[2,2048,320]{1,2,0:T(8,128)(2,1)}) %all-gather.7.cloned.1.call-update) | async-done | bytes 2621456 | tf_op jit(solution)/shard_map/all_gather | solution.py:30
  196.5 1.9 fusion.141
  198.4 27.2 %while.28 = (s32[]{:T(128)}, bf16[5,1,256,3,64]{2,4,3,1,0:T(8,128)(2,1)}, f32[5,1,3,256,1]{3,2,4,1,0:T(4,128)S(1)}, bf16[5,1,2048,64]{2,3,1,0:T(8,128)(2,1)S(1)}...) while((s32[]{:T(128)}, ...), condition=%wide.region_4.5_spmd.clone, body=%wide.region_1.4_spmd.clone.sunk | while | flops 420527616 | bytes 21726308 | solution.py:186
  201.5 2.4 fusion.186
  206.9 2.4 fusion.186
  212.3 2.4 fusion.186
  217.8 2.4 fusion.186
  223.2 2.4 fusion.186
  225.6 5.3 multiply_reduce_fusion.2
  230.9 51.5 %all-gather.13.cloned.1.call-done = bf16[16,60,5121]{2,1,0:T(8,128)(2,1)} async-done(((bf16[1,60,5121]{2,1,0:T(8,128)(2,1)}), bf16[16,60,5121]{2,1,0:T(8,128)(2,1)}) %all-gather.13.cloned.1.call-update) | async-done | bytes 9832336 | tf_op jit(solution)/shard_map/all_gather | solution.py:22
  282.4 11.8 %reshape.611 = bf16[960,5121]{1,0:T(8,128)(2,1)} reshape(bf16[16,60,5121]{2,1,0:T(8,128)(2,1)} %all-gather.13.cloned.1.call-done) | data formatting | bytes 19664640
  295.3 1.5 multiply_convert_fusion.3
  296.9 4.8 fusion.77
  301.7 6.0 multiply_convert_fusion.1
  307.7 2.2 fusion.75
  309.9 2.9 multiply_reduce_fusion
  313.1 3.3 fusion.97
  316.4 58.9 %while.29 = (s32[]{:T(128)}, f32[5,1,256,3,64]{2,4,3,1,0:T(8,128)}, bf16[5,1,2048,64]{2,3,1,0:T(8,128)(2,1)}, bf16[5,1,2048,64]{2,3,1,0:T(8,128)(2,1)}, bf16[5,1...) while((s32[]{:T(128)}, f32[5,1,256,3,64]{2,4,3,1,0:T(8,128)}, ...), condition=%wide.region_9.10_spmd.clone, body=%wide.region_7.9_spmd.clone.sunk | while | flops 1021492736 | bytes 61168820 | solution.py:251
  317.2 2.0 fusion.195
  319.2 2.0 fusion.196
  322.4 2.7 fusion.200
  328.9 2.0 fusion.195
  330.9 2.0 fusion.196
  334.1 2.7 fusion.200
  340.6 2.0 fusion.195
  342.6 2.0 fusion.196
  345.8 2.7 fusion.200
  352.3 2.0 fusion.195
  354.3 2.0 fusion.196
  357.4 2.7 fusion.200
  363.9 2.0 fusion.195
  365.9 2.0 fusion.196
  369.1 2.7 fusion.200
  375.3 3.4 pad_maximum_fusion
  380.1 3.9 convolution_convert_fusion
  388.0 2.0 convolution_convert_fusion.4
  390.0 3.5 fusion.88
  393.5 2.0 convolution_convert_fusion.3
  395.4 3.7 convolution_convert_fusion.2
  399.1 3.7 convolution_convert_fusion.1
  402.8 36.2 %reduce-scatter.15.cloned.1.call-done = bf16[2,256,320]{1,2,0:T(8,128)(2,1)} async-done(((bf16[2,2048,320]{1,2,0:T(8,128)(2,1)}), bf16[2,256,320]{1,2,0:T(8,128)(2,1)}) %reduce-scatter.15.cloned.1.call-update) | async-done | bytes 327696 | tf_op jit(solution)/shard_map/reduce_scatter | solution.py:41
  442.9 102.4 %fusion.140 = (bf16[64,960]{1,0:T(8,128)(2,1)S(1)}, bf16[64,320]{1,0:T(8,128)(2,1)S(1)}, bf16[64,320]{1,0:T(8,128)(2,1)S(1)}, bf16[64,960]{1,0:T(8,128)(2,1)S(1)...) fusion(bf16[960,960]{1,0:T(8,128)(2,1)} %convolution_convert_fusion.4, ...), kind=kCustom, calls=%all-reduce-scatter.6 | all-reduce-scatter fusion | flops 7864321 | bytes 15729152
  545.3 2.0 collective-permute-start.2
  547.4 1.7 convolution_add_fusion.1
  549.1 2.7 fusion.114
  551.8 34.4 %all-reduce.14 = (bf16[960]{0:T(1024)(128)(2,1)S(1)}, bf16[960]{0:T(1024)(128)(2,1)S(1)}) all-reduce(bf16[960]{0:T(1024)(128)(2,1)S(1)} %get-tuple-element.150, bf16[960]{0:T(1024)(128)(2,1)S(1)} %copy-done.31), channel_id=3, replica_groups=mesh['fsdp'=16,'ctx'=8] {'fsdp'}, use_global_device_ids=true, to_apply=%region_13.14.clone | all-reduce | flops 1920 | bytes 7680
  587.7 2.0 collective-permute-start.3
  589.7 1.9 collective-permute-start
  593.3 2.0 collective-permute-start.5
  595.3 2.8 collective-permute-start.4
  603.3 2.5 concatenate.76
  610.5 20.0 %concatenate.70 = bf16[614520]{0:T(1024)(128)(2,1)} concatenate(bf16[60]{0:T(256)(128)(2,1)S(1)} %dynamic-slice.1, bf16[57600]{0:T(1024)(128)(2,1)S(1)} %reshape.590, bf16[19200]{0:T(1024)(128)(2,1)S(1)} %copy-done.24, bf16[19200]{0:T(1024)(128)(2,1)S(1)} %reshape.592, bf16[57600]{0:T(1024)(128)(2,1)S(1)} %reshape.593, bf16[60]{0:T(256)(128)(2,1)S(1)} %dynamic-slice.11, ...), dimensions={0} | concatenate | bytes 2458080 | tf_op jit(solution)/shard_map/concatenate | solution.py:46
  630.6 5.9 fusion.106
  637.5 81.2 %all-reduce.18.cloned.1.call-done = bf16[614520]{0:T(1024)(128)(2,1)} async-done(((bf16[614520]{0:T(1024)(128)(2,1)}), bf16[614520]{0:T(1024)(128)(2,1)}) %all-reduce.18.cloned.1.call-update) | async-done | bytes 1229056 | tf_op jit(solution)/shard_map/psum | solution.py:47
  (234 shorter events, 79.8 us)
Async XLA Ops:
  7.2 67.2 %all-gather.11.cloned.1.call-start = ((), (), s32[]{:S(2)}) async-start(), calls=%async_computation.7 | async-start | bytes 5849088 | tf_op jit(solution)/shard_map/all_gather | solution.py:22
  10.0 125.5 %all-gather.9.cloned.1.call-start = ((), (), s32[]{:S(2)}) async-start(), calls=%async_computation.3 | async-start | bytes 5570560 | tf_op jit(solution)/shard_map/all_gather | solution.py:193
  10.8 185.7 %all-gather.7.cloned.1.call-start = ((), (), s32[]{:S(2)}) async-start(), calls=%async_computation.2 | async-start | bytes 2949120 | tf_op jit(solution)/shard_map/all_gather | solution.py:30
  12.1 429.5 %copy-start.29 = (f32[256]{0:T(256)}, f32[256]{0:T(256)S(1)}, u32[]{:S(2)}) copy-start(f32[256]{0:T(256)S(1)} %add_rsqrt_fusion.1) | copy-start | bytes 3076
  82.4 3.0 copy-start.2
  85.3 356.2 %copy-start.27 = (f32[960]{0:T(1024)}, f32[960]{0:T(1024)S(1)}, u32[]{:S(2)}) copy-start(f32[960]{0:T(1024)S(1)} %convert_reduce_fusion.1) | copy-start | bytes 11524
  85.3 3.8 copy-start.33
  85.4 3.9 copy-start.22
  85.4 3.9 copy-start.23
  85.9 49.7 %copy-start.7 = (bf16[1,256,960]{1,2,0:T(8,128)(2,1)S(1)}, bf16[1,256,960]{1,2,0:T(8,128)(2,1)}, u32[]{:S(2)}) copy-start(bf16[1,256,960]{1,2,0:T(8,128)(2,1)} %param.25) | copy-start | bytes 1474564
  89.1 193.3 %all-gather.13.cloned.1.call-start = ((), (), s32[]{:S(2)}) async-start(), calls=%async_computation.8 | async-start | bytes 11419648 | tf_op jit(solution)/shard_map/all_gather | solution.py:22
  90.7 348.4 %reduce-scatter.15.cloned.1.call-start = ((), (), s32[]{:S(2)}) async-start(), calls=%async_computation.4 | async-start | bytes 2949120 | tf_op jit(solution)/shard_map/reduce_scatter | solution.py:41
  225.6 68.6 %copy-start.1 = (bf16[5,1,2048,64]{2,3,1,0:T(8,128)(2,1)}, bf16[5,1,2048,64]{2,3,1,0:T(8,128)(2,1)S(1)}, u32[]{:S(2)}) copy-start(bf16[5,1,2048,64]{2,3,1,0:T(8,128)(2,1)S(1)} %get-tuple-element.423) | copy-start | bytes 3932164
  295.3 6.4 copy-start
  307.6 2.2 copy-start.12
  307.6 2.2 copy-start.14
  307.6 2.2 copy-start.4
  309.9 2.9 copy-start.8
  325.1 1.3 copy-start.10
  327.5 1.1 copy-start.11
  336.8 1.3 copy-start.10
  339.1 1.1 copy-start.11
  348.4 1.3 copy-start.10
  350.8 1.1 copy-start.11
  360.1 1.3 copy-start.10
  362.5 1.1 copy-start.11
  371.8 1.3 copy-start.10
  374.2 1.1 copy-start.11
  378.7 1.3 copy-start.6
  378.7 1.4 copy-start.9
  378.7 230.4 %reduce-scatter.17.cloned.1.call-start = ((), (), s32[]{:S(2)}) async-start(), calls=%async_computation.5 | async-start | bytes 5570560 | tf_op jit(solution)/shard_map/reduce_scatter | solution.py:346
  384.1 0.7 copy-start.32
  384.1 3.9 copy-start.3
  384.1 334.6 %all-reduce.18.cloned.1.call-start = ((), (), s32[]{:S(2)}) async-start(), calls=%async_computation.6 | async-start | bytes 2461696 | tf_op jit(solution)/shard_map/psum | solution.py:47
  390.0 3.5 copy-start.21
  393.5 2.0 copy-start.15
  395.4 3.7 copy-start.13
  439.1 2.5 copy-start.25
  440.2 1.3 copy-start.20
  442.9 104.5 %copy-start.19 = (f32[256,960]{0,1:T(8,128)S(1)}, f32[256,960]{0,1:T(8,128)}, u32[]{:S(2)}) copy-start(f32[256,960]{0,1:T(8,128)} %fusion.88) | copy-start | bytes 2949124
  545.3 3.8 copy-start.26
  545.3 3.8 copy-start.28
  545.3 3.8 copy-start.30
  545.3 6.5 copy-start.31
  545.3 49.9 %collective-permute-start.2 = (bf16[60,320]{1,0:T(8,128)(2,1)S(1)}, bf16[60,320]{1,0:T(8,128)(2,1)}, u32[]{:S(2)}, u32[]{:S(2)}) collective-permute-start(bf16[60,320]{1,0:T(8,128)(2,1)S(1)} %slice.87), channel_id=1, source_target_pairs={{0,8},{8,16},{16,24},{24,32},{32,40},{40,48},{48,56},{56,64},{64,7... | collective-permute-start | bytes 115208
  586.3 13.0 %collective-permute-start.1 = (bf16[60,320]{1,0:T(8,128)(2,1)S(1)}, bf16[60,320]{1,0:T(8,128)(2,1)S(1)}, u32[]{:S(2)}, u32[]{:S(2)}) collective-permute-start(bf16[60,320]{1,0:T(8,128)(2,1)S(1)} %slice.86), channel_id=1, source_target_pairs={{0,8},{8,16},{16,24},{24,32},{32,40},{40,48},{48,56},{56,64},{64,7... | collective-permute-start | bytes 115208
  587.7 12.8 %collective-permute-start.3 = (bf16[60,960]{1,0:T(8,128)(2,1)S(1)}, bf16[60,960]{1,0:T(8,128)(2,1)}, u32[]{:S(2)}, u32[]{:S(2)}) collective-permute-start(bf16[60,960]{1,0:T(8,128)(2,1)S(1)} %slice.88), channel_id=1, source_target_pairs={{0,8},{8,16},{16,24},{24,32},{32,40},{40,48},{48,56},{56,64},{64,7... | collective-permute-start | bytes 345608
  589.7 12.2 %collective-permute-start = (bf16[60,960]{1,0:T(8,128)(2,1)S(1)}, bf16[60,960]{1,0:T(8,128)(2,1)}, u32[]{:S(2)}, u32[]{:S(2)}) collective-permute-start(bf16[60,960]{1,0:T(8,128)(2,1)S(1)} %slice.85), channel_id=1, source_target_pairs={{0,8},{8,16},{16,24},{24,32},{32,40},{40,48},{48,56},{56,64},{64,7... | collective-permute-start | bytes 345608
  593.3 10.1 %collective-permute-start.5 = (bf16[60,2560]{1,0:T(8,128)(2,1)}, bf16[60,2560]{1,0:T(8,128)(2,1)}, u32[]{:S(2)}, u32[]{:S(2)}) collective-permute-start(bf16[60,2560]{1,0:T(8,128)(2,1)} %slice.90), channel_id=1, source_target_pairs={{0,8},{8,16},{16,24},{24,32},{32,40},{40,48},{48,56},{56,64},{64,7... | collective-permute-start | bytes 921608
  595.3 11.8 %collective-permute-start.4 = (bf16[60,2560]{1,0:T(8,128)(2,1)}, bf16[60,2560]{1,0:T(8,128)(2,1)S(1)}, u32[]{:S(2)}, u32[]{:S(2)}) collective-permute-start(bf16[60,2560]{1,0:T(8,128)(2,1)} %slice.89), channel_id=1, source_target_pairs={{0,8},{8,16},{16,24},{24,32},{32,40},{40,48},{48,56},{56,64},{64,7... | collective-permute-start | bytes 921608
  603.3 7.2 copy-start.24
  607.0 3.5 copy-start.17
  608.0 22.6 %copy-start.5 = (f32[256,960]{0,1:T(8,128)S(1)}, f32[256,960]{0,1:T(8,128)}, u32[]{:S(2)}) copy-start(f32[256,960]{0,1:T(8,128)} %get-tuple-element.233) | copy-start | bytes 2949124
  630.6 5.9 copy-start.18
  718.7 5.2 copy-start.16
Sparse Core Ops, SparseCore 0:
  11.0 63.3 all-gather.10
  76.8 58.6 all-gather.8
  137.7 58.7 all-gather.6
  198.8 83.5 all-gather.12
  378.9 60.1 reduce-scatter.14
  443.0 141.2 reduce-scatter.16
  630.7 87.9 all-reduce.17
where the time goes:
time: 742 us; the launch traced here: 735 us
  waiting for transfers between devices  324 us (44%)
  blocking collectives  137 us (18%)
  matrix products  130 us (18%)
  local copies, waits for them, and re-layouts  82.1 us (11%)
  other arithmetic  31.8 us (4%)
  between operations  16.4 us (2%)
  starting transfers between devices  12.5 us (2%)
    unnamed x2, blocking collectives  137 us
    all_gather x2, waiting for transfers between devices, side_by_side(): out = lax.all_gather(both, axis, axis=dim, tiled=True)  114 us
    psum x1, waiting for transfers between devices, packed_total(): running = lax.psum(line, axis)  81.2 us
    all_gather x1, waiting for transfers between devices, sent_together(): out = lax.all_gather(both, axis, axis=dim, tiled=True)  47.6 us
    all_gather x1, waiting for transfers between devices, on_device(): lax.all_gather(w_down, 'fsdp', axis=0, tiled=True)  44.8 us
    reduce_scatter x1, waiting for transfers between devices, side_by_side_2(): lax.psum_scatter(both, axis, scatter_dimension=dim, tiled=True)  36.2 us
    unnamed x87, local copies, waits for them, and re-layouts  31.6 us
    dot_general x7, matrix products, linear_projection(): return jnp.dot(left, right, preferred_element_type=jnp.float32)  27 us
  transfers between devices with their start and end apart: 13, of which 6 were waited for; matrix products, arithmetic and copies ran while one was open for 29% of the time, Pallas kernels for 0%

commit v1 on v0

v1 whole, which is shorter than its diff:
```python
import functools
import math

import jax
import jax.numpy as jnp
from jax import lax
from jax.experimental import pallas as pl
from jax.experimental.pallas import tpu as pltpu
from jax.sharding import PartitionSpec as P

QUERY_HEADS = 15
KEY_VALUE_HEADS = 5
HEAD_WIDTH = 64
GROUP = QUERY_HEADS // KEY_VALUE_HEADS
WIDTH = 960
ROWS = 60
PAD = 64
SHARDS = 16
PADDED = SHARDS * PAD
KV_WIDTH = KEY_VALUE_HEADS * HEAD_WIDTH
QKV_WIDTH = 1664

EPS = 1e-05
ROPE_BASE = 10000.0
MESH = pl.DeviceIdType.MESH
BF16 = jnp.bfloat16
F32 = jnp.float32


def place():
    f, t = lax.axis_index("fsdp"), lax.axis_index("ctx")
    return f // 8, (f // 2) % 4, f % 2, t // 2, t % 2


def device(yh, x, c, z, yl):
    return ((yh * 4 + x) * 2 + c, z * 2 + yl)


class Places:
    def __init__(self):
        yh, x, c, z, yl = place()
        self.yh, self.x, self.c, self.z, self.yl = yh, x, c, z, yl
        self.sib = device(yh, x, 1 - c, z, yl)
        self.ypair = device(1 - yh, x, c, z, 1 - yl)
        self.ylo = device(yh, x, c, z, 1 - yl)
        self.xs = [(x + 1) % 4, (x + 3) % 4, (x + 2) % 4]
        self.zs = [(z + 1) % 4, (z + 3) % 4, (z + 2) % 4]
        self.xdev = [device(yh, k, c, z, yl) for k in self.xs]
        self.zdev = [device(yh, x, c, k, yl) for k in self.zs]
        self.xfrom = [self.xs[1], self.xs[0], self.xs[2]]
        self.zfrom = [self.zs[1], self.zs[0], self.zs[2]]


def greet(devices):
    barrier = pltpu.get_barrier_semaphore()
    for d in devices:
        pl.semaphore_signal(barrier, inc=1, device_id=d, device_id_type=MESH)
    pl.semaphore_wait(barrier, len(devices))


class Sems:
    def __init__(self, send, recv):
        self.send, self.recv, self.at, self.open = send, recv, 0, []

    def take(self, count=1):
        at = self.at
        self.at += count
        return at

    def push(self, slot, src, dst, dev):
        copy = pltpu.make_async_remote_copy(
            src_ref=src,
            dst_ref=dst,
            send_sem=self.send.at[slot],
            recv_sem=self.recv.at[slot],
            device_id=dev,
            device_id_type=MESH,
        )
        copy.start()
        self.open.append(copy)

    def arrived(self, slot, dst, dev):
        pltpu.make_async_remote_copy(
            src_ref=dst,
            dst_ref=dst,
            send_sem=self.send.at[slot],
            recv_sem=self.recv.at[slot],
            device_id=dev,
            device_id_type=MESH,
        ).wait_recv()

    def finish(self):
        for copy in self.open:
            copy.wait_send()
        self.open = []


GATHER_SEMS = 24


def gather_steps(pc, sems, local_sem, shard, out, split):
    rows = shard.shape[0]
    quarter = rows // 4
    yh, x, c, z = pc.yh, pc.x, pc.c, pc.z
    s_y = sems.take()
    s_x = [[sems.take() for _ in range(2)] for _ in range(3)]
    s_z = [[sems.take() for _ in range(3)] for _ in range(3)] if split else None
    s_s = [sems.take() for _ in range(4)]
    band = pl.ds(pl.multiple_of(z * quarter, 16), quarter) if split else pl.ds(0, rows)

    own = pltpu.make_async_copy(shard, out.at[yh, x, c], local_sem)
    own.start()
    sems.push(s_y, shard, out.at[yh, x, c], pc.ypair)
    for k in (0, 1, 2):
        sems.push(s_x[k][0], shard.at[band], out.at[yh, x, c, band], pc.xdev[k])
    yield
    sems.arrived(s_y, out.at[1 - yh, x, c], pc.ypair)
    for k in (0, 1, 2):
        piece = out.at[1 - yh, x, c, band]
        sems.push(s_x[k][1], piece, piece, pc.xdev[k])
    own.wait()
    sems.push(s_s[3], out.at[:, x, c], out.at[:, x, c], pc.sib)
    yield
    for k in (0, 1, 2):
        far = pc.xfrom[k]
        sems.arrived(s_x[k][0], out.at[yh, far, c, band], pc.xdev[k])
        sems.arrived(s_x[k][1], out.at[1 - yh, far, c, band], pc.xdev[k])
        if split:
            piece = out.at[:, far, c, band]
            for j in range(3):
                sems.push(s_z[k][j], piece, piece, pc.zdev[j])
        else:
            sems.push(s_s[k], out.at[:, far, c], out.at[:, far, c], pc.sib)
    yield
    if split:
        for k in (0, 1, 2):
            far = pc.xfrom[k]
            for j in range(3):
                there = pl.ds(pl.multiple_of(pc.zfrom[j] * quarter, 16), quarter)
                sems.arrived(s_z[k][j], out.at[:, far, c, there], pc.zdev[j])
            sems.push(s_s[k], out.at[:, far, c], out.at[:, far, c], pc.sib)
        yield
    for k in (0, 1, 2, 3):
        far = x if k == 3 else pc.xfrom[k]
        sems.arrived(s_s[k], out.at[:, far, 1 - c], pc.sib)
    yield


def run_all(steps):
    live = list(steps)
    while live:
        for s in list(live):
            try:
                next(s)
            except StopIteration:
                live.remove(s)


def gather_kernel(splits, *refs):
    n = len(splits)
    shards, outs = refs[:n], refs[n : 2 * n]
    send, recv, local = refs[2 * n :]
    pc = Places()
    greet([pc.sib, pc.ypair, *pc.xdev, *pc.zdev])
    sems = Sems(send, recv)
    run_all(
        [
            gather_steps(pc, sems, local.at[k], shards[k], outs[k], splits[k])
            for k in range(n)
        ]
    )
    sems.finish()


def gather_weights(shards, splits, collective_id):
    n = len(shards)
    return pl.pallas_call(
        functools.partial(gather_kernel, splits),
        out_shape=[jax.ShapeDtypeStruct((2, 4, 2, *s.shape), s.dtype) for s in shards],
        in_specs=[pl.BlockSpec(memory_space=pl.ANY)] * n,
        out_specs=[pl.BlockSpec(memory_space=pl.ANY)] * n,
        scratch_shapes=[
            pltpu.SemaphoreType.DMA((n * GATHER_SEMS,)),
            pltpu.SemaphoreType.DMA((n * GATHER_SEMS,)),
            pltpu.SemaphoreType.DMA((n,)),
        ],
        compiler_params=pltpu.CompilerParams(
            collective_id=collective_id, has_side_effects=True, vmem_limit_bytes=60 << 20
        ),
    )(*shards)


REDUCE_SEMS = 24


def add_rows(dst, terms, shape):
    lead, rows = shape[:-2], shape[-2]
    blocks = rows // 16
    count = math.prod(lead) * blocks

    def body(i, carry):
        idx, rest = [], i // blocks
        for size in reversed(lead):
            idx.append(rest % size)
            rest = rest // size
        idx = tuple(reversed(idx))
        at = (*idx, pl.ds(pl.multiple_of((i % blocks) * 16, 16), 16))
        total = dst[at].astype(F32)
        for term in terms:
            total = total + term[at].astype(F32)
        dst[at] = total.astype(BF16)
        return carry

    lax.fori_loop(0, count, body, 0)


def reduce_scratch(rows, width, split):
    q = rows // 4
    buffers = [pltpu.VMEM((2, 4, rows, width), BF16)] * 2
    if split:
        buffers += [
            pltpu.VMEM((3, 2, 4, q, width), BF16),
            pltpu.VMEM((3, 2, q, width), BF16),
            pltpu.VMEM((q, width), BF16),
            pltpu.VMEM((q, width), BF16),
        ]
    else:
        w = width // 4
        buffers += [
            pltpu.VMEM((3, rows, w), BF16),
            pltpu.VMEM((3, 2, rows, width), BF16),
            pltpu.VMEM((rows, width), BF16),
            pltpu.VMEM((rows, w), BF16),
        ]
    return buffers


def reduce_steps(pc, sems, local_sem, part, final, buffers, split):
    yh, x, c, z = pc.yh, pc.x, pc.c, pc.z
    acc, from_sib, from_z, from_x, from_y, from_l = buffers
    rows, width = part.shape[-2:]
    s_s, s_y, s_l = sems.take(), sems.take(), sems.take()
    s_x = [sems.take() for _ in range(3)]
    s_z = [sems.take() for _ in range(3)]
    s_f = [sems.take() for _ in range(3)]
    if split:
        q = rows // 4

        def band(k):
            return (pl.ds(pl.multiple_of(k * q, 16), q), slice(None))
    else:
        q = width // 4

        def band(k):
            return (slice(None), pl.ds(pl.multiple_of(k * q, 128), q))

    here = band(z)
    sems.push(s_s, part.at[:, :, 1 - c], from_sib, pc.sib)
    own = pltpu.make_async_copy(part.at[:, :, c], acc, local_sem)
    own.start()
    yield
    own.wait()
    sems.arrived(s_s, from_sib, pc.sib)
    add_rows(acc, [from_sib], acc.shape)
    if split:
        for j in range(3):
            there = band(pc.zs[j])
            sems.push(s_z[j], acc.at[:, :, *there], from_z.at[j], pc.zdev[j])
        yield
        for j in range(3):
            sems.arrived(s_z[j], from_z.at[j], pc.zdev[j])
        mine = acc.at[:, :, *here]
        add_rows(mine, [from_z.at[j] for j in range(3)], (2, 4, q, width))
        for k in range(3):
            sems.push(s_x[k], acc.at[:, pc.xs[k], *here], from_x.at[k], pc.xdev[k])
        yield
        for k in range(3):
            sems.arrived(s_x[k], from_x.at[k], pc.xdev[k])
        add_rows(acc.at[:, x, *here], [from_x.at[k] for k in range(3)], (2, q, width))
        sems.push(s_y, acc.at[1 - yh, x, *here], from_y, pc.ypair)
        yield
        sems.arrived(s_y, from_y, pc.ypair)
        mine = acc.at[yh, x, *here]
        add_rows(mine, [from_y], (q, width))
    else:
        for k in range(3):
            sems.push(s_x[k], acc.at[:, pc.xs[k]], from_x.at[k], pc.xdev[k])
        yield
        for k in range(3):
            sems.arrived(s_x[k], from_x.at[k], pc.xdev[k])
        add_rows(acc.at[:, x], [from_x.at[k] for k in range(3)], (2, rows, width))
        sems.push(s_y, acc.at[1 - yh, x], from_y, pc.ypair)
        yield
        sems.arrived(s_y, from_y, pc.ypair)
        add_rows(acc.at[yh, x], [from_y], (rows, width))
        for j in range(3):
            there = band(pc.zs[j])
            sems.push(s_z[j], acc.at[yh, x, *there], from_z.at[j], pc.zdev[j])
        yield
        for j in range(3):
            sems.arrived(s_z[j], from_z.at[j], pc.zdev[j])
        mine = acc.at[yh, x, *here]
        add_rows(mine, [from_z.at[j] for j in range(3)], (rows, q))
    sems.push(s_l, mine, from_l, pc.ylo)
    yield
    sems.arrived(s_l, from_l, pc.ylo)
    final[here] = (mine[...].astype(F32) + from_l[...].astype(F32)).astype(BF16)
    for j in range(3):
        sems.push(s_f[j], final.at[here], final.at[here], pc.zdev[j])
    yield
    for j in range(3):
        sems.arrived(s_f[j], final.at[band(pc.zfrom[j])], pc.zdev[j])
    yield


def reduce_kernel(splits, *refs):
    n = len(splits)
    parts, finals = refs[:n], refs[n : 2 * n]
    scratch = refs[2 * n :]
    send, recv, local = scratch[:3]
    buffers = [scratch[3 + 6 * k : 9 + 6 * k] for k in range(n)]
    pc = Places()
    greet([pc.sib, pc.ypair, pc.ylo, *pc.xdev, *pc.zdev])
    sems = Sems(send, recv)
    run_all(
        [
            reduce_steps(pc, sems, local.at[k], parts[k], finals[k], buffers[k], splits[k])
            for k in range(n)
        ]
    )
    sems.finish()


def reduce_grads(parts, splits, collective_id):
    n = len(parts)
    scratch = [
        pltpu.SemaphoreType.DMA((n * REDUCE_SEMS,)),
        pltpu.SemaphoreType.DMA((n * REDUCE_SEMS,)),
        pltpu.SemaphoreType.DMA((n,)),
    ]
    for p, s in zip(parts, splits):
        scratch += reduce_scratch(*p.shape[-2:], s)
    return pl.pallas_call(
        functools.partial(reduce_kernel, splits),
        out_shape=[jax.ShapeDtypeStruct(p.shape[-2:], p.dtype) for p in parts],
        in_specs=[pl.BlockSpec(memory_space=pl.ANY)] * n,
        out_specs=[pl.BlockSpec(memory_space=pltpu.VMEM)] * n,
        scratch_shapes=scratch,
        compiler_params=pltpu.CompilerParams(
            collective_id=collective_id, has_side_effects=True, vmem_limit_bytes=60 << 20
        ),
    )(*parts)


def ctx_places():
    f, t = lax.axis_index("fsdp"), lax.axis_index("ctx")
    return t, [((t + k) % 8, (f, (t + k) % 8)) for k in range(1, 8)]


def spread_kernel(block, out, send, recv, local):
    t, others = ctx_places()
    greet([d for _, d in others])
    sems = Sems(send, recv)
    own = pltpu.make_async_copy(block, out.at[t], local)
    own.start()
    for k, (_, d) in enumerate(others):
        sems.push(k, block, out.at[t], d)
    own.wait()
    for k in range(7):
        source, d = others[6 - k]
        sems.arrived(k, out.at[source], d)
    sems.finish()


def spread_blocks(block, collective_id):
    return pl.pallas_call(
        spread_kernel,
        out_shape=jax.ShapeDtypeStruct((8, *block.shape), block.dtype),
        in_specs=[pl.BlockSpec(memory_space=pl.ANY)],
        out_specs=pl.BlockSpec(memory_space=pl.ANY),
        scratch_shapes=[
            pltpu.SemaphoreType.DMA((7,)),
            pltpu.SemaphoreType.DMA((7,)),
            pltpu.SemaphoreType.DMA,
        ],
        compiler_params=pltpu.CompilerParams(
            collective_id=collective_id, has_side_effects=True, vmem_limit_bytes=60 << 20
        ),
    )(block)


def collect_kernel(parts, out, landed, send, recv):
    t, others = ctx_places()
    greet([d for _, d in others])
    sems = Sems(send, recv)
    for k, (there, d) in enumerate(others):
        sems.push(k, parts.at[there], landed.at[k], d)
    for k in range(7):
        sems.arrived(k, landed.at[k], others[6 - k][1])
    rows = out.shape[0]

    def body(i, carry):
        at = pl.ds(pl.multiple_of(i * 16, 16), 16)
        total = parts[t, at].astype(F32)
        for k in range(7):
            total = total + landed[k, at].astype(F32)
        out[at] = total
        return carry

    lax.fori_loop(0, rows // 16, body, 0)
    sems.finish()


def collect_blocks(parts, collective_id):
    return pl.pallas_call(
        collect_kernel,
        out_shape=jax.ShapeDtypeStruct(parts.shape[1:], F32),
        in_specs=[pl.BlockSpec(memory_space=pltpu.VMEM)],
        out_specs=pl.BlockSpec(memory_space=pltpu.VMEM),
        scratch_shapes=[
            pltpu.VMEM((7, *parts.shape[1:]), parts.dtype),
            pltpu.SemaphoreType.DMA((7,)),
            pltpu.SemaphoreType.DMA((7,)),
        ],
        compiler_params=pltpu.CompilerParams(
            collective_id=collective_id, has_side_effects=True, vmem_limit_bytes=60 << 20
        ),
    )(parts)


def rotary_tables(token_positions):
    half = HEAD_WIDTH // 2
    freqs = ROPE_BASE ** (-jnp.arange(half, dtype=F32) * 2.0 / HEAD_WIDTH)
    angles = token_positions.astype(F32)[:, None] * freqs[None, :]
    return jnp.cos(angles)[:, None, :], jnp.sin(angles)[:, None, :]


def rotate(rows, cosine, sine):
    half = HEAD_WIDTH // 2
    heads = rows.reshape(rows.shape[0], -1, HEAD_WIDTH)
    a, b = heads[..., :half], heads[..., half:]
    out = jnp.concatenate([a * cosine - b * sine, b * cosine + a * sine], axis=-1)
    return out.reshape(rows.shape)


def dot(a, b):
    return jnp.dot(a, b, preferred_element_type=F32)


def dot_tn(a, b):
    return lax.dot_general(a, b, (((0,), (0,)), ((), ())), preferred_element_type=F32)


def dot_nt(a, b):
    return lax.dot_general(a, b, (((1,), (1,)), ((), ())), preferred_element_type=F32)


def norm_scale(rows):
    return lax.rsqrt(jnp.sum(rows * rows, axis=-1, keepdims=True) * (1.0 / WIDTH) + EPS)


def norm_back(grad_normed, rows, scale, gain):
    unit = rows * scale
    grad_gain = jnp.sum(grad_normed * unit, axis=0)
    grad_unit = grad_normed * gain
    mean = jnp.sum(grad_unit * unit, axis=-1, keepdims=True) * (1.0 / WIDTH)
    return scale * (grad_unit - unit * mean), grad_gain


def head_scores(query_head, keys_head, token_positions):
    scores = jnp.einsum("gle,me->glm", query_head, keys_head, preferred_element_type=F32)
    scores = scores * HEAD_WIDTH ** (-0.5)
    causal = token_positions[:, None] >= jnp.arange(keys_head.shape[0], dtype=jnp.int32)[None, :]
    return jnp.where(causal, scores, -1e30)


def split_heads(rows):
    return jnp.moveaxis(rows.reshape(rows.shape[0], KEY_VALUE_HEADS, GROUP, HEAD_WIDTH), 0, 2)


def join_heads(heads):
    return jnp.moveaxis(heads, 2, 0).reshape(heads.shape[2], QUERY_HEADS * HEAD_WIDTH)


def on_device(
    tokens,
    attn_gain,
    w_query,
    key_weight,
    value_weight,
    w_out,
    ffn_gain,
    w_gate,
    w_up,
    w_down,
    d_out,
):
    block = tokens.shape[1]
    token_positions = lax.axis_index("ctx") * block + jnp.arange(block, dtype=jnp.int32)
    cosine, sine = rotary_tables(token_positions)
    factor = HEAD_WIDTH ** (-0.5)
    feature = jnp.arange(WIDTH, dtype=jnp.int32)
    place_of = feature // ROWS * PAD + feature % ROWS
    select = (place_of[:, None] == jnp.arange(PADDED, dtype=jnp.int32)[None, :]).astype(BF16)

    pad_rows = ((0, PAD - ROWS), (0, 0))
    qkv_shard = jnp.pad(
        jnp.concatenate(
            [w_query, key_weight, value_weight, attn_gain[:, None], ffn_gain[:, None]], axis=1
        ),
        ((0, PAD - ROWS), (0, QKV_WIDTH - WIDTH - 2 * KV_WIDTH - 2)),
    )
    out_shard = jnp.pad(dot(w_out, select).astype(BF16), pad_rows)
    gate_shard = jnp.pad(w_gate, pad_rows)
    up_shard = jnp.pad(w_up, pad_rows)
    down_shard = dot(w_down, select).astype(BF16)

    qkv_w, out_w = gather_weights((qkv_shard, out_shard), (True, False), 0)
    qkv_w, out_w = qkv_w.reshape(PADDED, QKV_WIDTH), out_w.reshape(PADDED, PADDED)
    gains = qkv_w[:, WIDTH + 2 * KV_WIDTH : WIDTH + 2 * KV_WIDTH + 2].astype(F32)
    gain_one, gain_two = gains[:, 0], gains[:, 1]

    flat = dot(tokens[0], select)
    grad_flat = dot(d_out[0], select).astype(BF16)
    scale_one = norm_scale(flat)
    normed = (flat * scale_one * gain_one).astype(BF16)
    qkv = dot(normed, qkv_w)
    query = rotate(qkv[:, :WIDTH], cosine, sine).astype(BF16)
    keys = rotate(qkv[:, WIDTH : WIDTH + KV_WIDTH], cosine, sine).astype(BF16)
    values = qkv[:, WIDTH + KV_WIDTH : WIDTH + 2 * KV_WIDTH].astype(BF16)
    kv = spread_blocks(jnp.concatenate([keys, values], axis=1), 1)
    kv = kv.reshape(8 * block, 2 * KV_WIDTH)
    gate_w, up_w, down_w = gather_weights(
        (gate_shard, up_shard, down_shard), (True, True, False), 2
    )
    gate_w, up_w = gate_w.reshape(PADDED, -1), up_w.reshape(PADDED, -1)
    down_w = down_w.reshape(-1, PADDED)

    query_heads = split_heads(query)
    kv_heads = jnp.moveaxis(kv.reshape(8 * block, 2, KEY_VALUE_HEADS, HEAD_WIDTH), 0, 2)
    keys_heads, values_heads = kv_heads[0], kv_heads[1]

    def head_forward(operands):
        query_head, keys_head, values_head = operands
        scores = head_scores(query_head, keys_head, token_positions)
        peak = jnp.max(scores, axis=-1, keepdims=True)
        logsum = peak + jnp.log(jnp.sum(jnp.exp(scores - peak), axis=-1, keepdims=True))
        probs_low = jnp.exp(scores - logsum).astype(BF16)
        mixed = jnp.einsum("glm,me->gle", probs_low, values_head, preferred_element_type=F32)
        return mixed.astype(BF16), logsum

    mixed_heads, logsums = lax.map(head_forward, (query_heads, keys_heads, values_heads))
    mixed = dot(join_heads(mixed_heads), select).astype(BF16)

    resid = flat + dot(mixed, out_w)
    scale_two = norm_scale(resid)
    normed_two = (resid * scale_two * gain_two).astype(BF16)
    gate = dot(normed_two, gate_w)
    up = dot(normed_two, up_w)
    sigmoid = jax.nn.sigmoid(gate)
    swish = gate * sigmoid
    hidden = (swish * up).astype(BF16)
    output = (resid + dot(hidden, down_w)).astype(BF16)
    output = dot_nt(output, select).astype(BF16)
    grad_down = dot_tn(hidden, grad_flat)
    grad_hidden = dot_nt(grad_flat, down_w)
    grad_gate_v = (grad_hidden * up * sigmoid * (1.0 + gate * (1.0 - sigmoid))).astype(BF16)
    grad_up_v = (grad_hidden * swish).astype(BF16)
    grad_gate = dot_tn(normed_two, grad_gate_v)
    grad_up = dot_tn(normed_two, grad_up_v)
    grad_normed_two = dot_nt(grad_gate_v, gate_w) + dot_nt(grad_up_v, up_w)
    resid_term, grad_gain_two = norm_back(grad_normed_two, resid, scale_two, gain_two)
    grad_resid = grad_flat.astype(F32) + resid_term
    grad_branch = grad_resid.astype(BF16)
    grad_out = dot_tn(mixed, grad_branch)
    grad_mixed = dot_nt(dot_nt(grad_branch, out_w).astype(BF16), select).astype(BF16)
    ffn = (
        grad_gate.astype(BF16).reshape(2, 4, 2, PAD, -1),
        grad_up.astype(BF16).reshape(2, 4, 2, PAD, -1),
        grad_down.astype(BF16).reshape(2, 4, 2, -1, PADDED),
    )
    sum_gate, sum_up, sum_down = reduce_grads(ffn, (True, True, False), 3)

    def head_backward(operands):
        query_head, keys_head, values_head, grad_head, logsum = operands
        scores = head_scores(query_head, keys_head, token_positions)
        probs = jnp.exp(scores - logsum)
        probs_low = probs.astype(BF16)
        grad_probs = jnp.einsum("gle,me->glm", grad_head, values_head, preferred_element_type=F32)
        grad_values = jnp.einsum("glm,gle->me", probs_low, grad_head, preferred_element_type=F32)
        grad_scores = probs * (grad_probs - jnp.sum(probs * grad_probs, axis=-1, keepdims=True))
        grad_scores = grad_scores.astype(BF16)
        grad_query = jnp.einsum("glm,me->gle", grad_scores, keys_head, preferred_element_type=F32)
        grad_keys = jnp.einsum("glm,gle->me", grad_scores, query_head, preferred_element_type=F32)
        return grad_query * factor, grad_keys * factor, grad_values

    grad_query_heads, grad_keys_heads, grad_values_heads = lax.map(
        head_backward,
        (query_heads, keys_heads, values_heads, split_heads(grad_mixed), logsums),
    )
    grad_kv = jnp.stack([grad_keys_heads, grad_values_heads]).astype(BF16)
    grad_kv = jnp.moveaxis(grad_kv, 2, 0).reshape(8, block, 2 * KV_WIDTH)
    grad_kv = collect_blocks(grad_kv, 4)
    grad_query = rotate(join_heads(grad_query_heads), cosine, -sine)
    grad_keys = rotate(grad_kv[:, :KV_WIDTH], cosine, -sine)
    grad_qkv = jnp.concatenate([grad_query, grad_keys, grad_kv[:, KV_WIDTH:]], axis=1).astype(BF16)
    grad_qkv_w = dot_tn(normed, grad_qkv)
    grad_normed = dot_nt(grad_qkv, qkv_w[:, : WIDTH + 2 * KV_WIDTH])
    token_term, grad_gain_one = norm_back(grad_normed, flat, scale_one, gain_one)
    d_tokens = dot_nt((grad_resid + token_term).astype(BF16), select).astype(BF16)
    qkv_part = jnp.concatenate(
        [
            grad_qkv_w,
            grad_gain_one[:, None],
            grad_gain_two[:, None],
            jnp.zeros((PADDED, QKV_WIDTH - WIDTH - 2 * KV_WIDTH - 2), F32),
        ],
        axis=1,
    ).astype(BF16)
    attn = (
        qkv_part.reshape(2, 4, 2, PAD, QKV_WIDTH),
        grad_out.astype(BF16).reshape(2, 4, 2, PAD, PADDED),
    )
    sum_qkv, sum_out = reduce_grads(attn, (True, False), 5)
    sum_qkv = sum_qkv[:ROWS].astype(F32)
    ends = (WIDTH, WIDTH + KV_WIDTH, WIDTH + 2 * KV_WIDTH)
    return (
        output[None],
        d_tokens[None],
        sum_qkv[:, ends[2]],
        sum_qkv[:, : ends[0]],
        sum_qkv[:, ends[0] : ends[1]],
        sum_qkv[:, ends[1] : ends[2]],
        dot_nt(sum_out[:ROWS], select),
        sum_qkv[:, ends[2] + 1],
        sum_gate[:ROWS].astype(F32),
        sum_up[:ROWS].astype(F32),
        dot_nt(sum_down, select),
    )


def solution(mesh):
    rows, whole, line = P("fsdp", None), P("fsdp", "ctx", None), P("fsdp")
    weights = (line, rows, rows, rows, rows, line, rows, rows, rows)
    return jax.shard_map(
        on_device,
        mesh=mesh,
        in_specs=(whole, *weights, whole),
        out_specs=(whole, whole, *weights),
        check_vma=False,
    )
```

time: 742 us -> 571 us (0.77)
  Pallas kernels: 0 us -> 334 us
  waiting for transfers between devices: 324 us -> 0 us
  blocking collectives: 137 us -> 0 us
  local copies, waits for them, and re-layouts: 82.1 us -> 52.9 us
  matrix products: 130 us -> 146 us
  between operations: 16.4 us -> 1.9 us
  starting transfers between devices: 12.5 us -> 0 us
    pallas_call x0 -> x6, Pallas kernels: none -> 334 us  [the longest x2 146 us: reduce_grads(): pl.pallas_call(functools.partial(reduce_kernel, splits), out_shape=[jax.S...]
    all_gather x4 -> x0, waiting for transfers between devices: 206 us -> none  [the longest x2 114 us: side_by_side(): out = lax.all_gather(both, axis, axis=dim, tiled=True)]
    unnamed x2 -> x0, blocking collectives: 137 us -> none
    psum x1 -> x0, waiting for transfers between devices: 81.2 us -> none  [packed_total(): running = lax.psum(line, axis)]
    reduce_scatter x2 -> x0, waiting for transfers between devices: 36.2 us -> none  [the longest x1 36.2 us: side_by_side_2(): lax.psum_scatter(both, axis, scatter_dimension=dim, tiled=True)]
    unnamed x87 -> x90, local copies, waits for them, and re-layouts: 31.6 us -> 7.02 us
    concatenate x3 -> x4, local copies, waits for them, and re-layouts: 23.4 us -> 7.55 us  [the longest x3 7.42 us: on_device(): jnp.concatenate([grad_qkv_w, grad_gain_one[:, None], grad_gain_two[:, Non...]
    dot_general x56 -> x58, matrix products: 130 us -> 146 us  [the longest x9 30.3 us: dot_nt(): lax.dot_general(a, b, (((1,), (1,)), ((), ())), preferred_element_type=F32)]
  transfers between devices with their start and end apart: 13 -> 0, of which waited for: 6 -> 0; matrix products, arithmetic and copies ran while one was open for 29% -> 0% of each run, Pallas kernels for 0% -> 0%
where the time goes in v1:
time: 571 us; the launch traced here: 560 us
  Pallas kernels  334 us (58%)
  matrix products  146 us (26%)
  local copies, waits for them, and re-layouts  52.9 us (9%)
  other arithmetic  25.2 us (4%)
    pallas_call x2, Pallas kernels, reduce_grads(): pl.pallas_call(functools.partial(reduce_kernel, splits), out_shape=[jax.S...  146 us
    pallas_call x2, Pallas kernels, gather_weights(): pl.pallas_call(functools.partial(gather_kernel, splits), out_shape=[jax.S...  117 us
    pallas_call x1, Pallas kernels, collect_blocks(): pl.pallas_call(collect_kernel, out_shape=jax.ShapeDtypeStruct(parts.shape...  36.3 us
    pallas_call x1, Pallas kernels, spread_blocks(): pl.pallas_call(spread_kernel, out_shape=jax.ShapeDtypeStruct((8, *block.s...  33.9 us
    dot_general x9, matrix products, dot_nt(): lax.dot_general(a, b, (((1,), (1,)), ((), ())), preferred_element_type=F32)  30.3 us
    dot_general x10, matrix products, head_scores(): jnp.einsum('gle,me->glm', query_head, keys_head, preferred_element_type=F32)  23 us
    dot_general x9, matrix products, dot(): return jnp.dot(a, b, preferred_element_type=F32)  17.4 us
    dot_general x5, matrix products, head_forward(): jnp.einsum('glm,me->gle', probs_low, values_head, preferred_element_type=...  16.9 us

profile of v1, /device:TPU:0, one launch (start us, length us, event | category | flops | bytes accessed | tf_op | source)
XLA Modules:
  0.0 560.2 jit_solution(7290971244574667229)
XLA Ops:
  5.8 36.0 %shard_map.194 = (bf16[2,4,2,64,1664]{4,3,2,1,0:T(8,128)(2,1)}, bf16[2,4,2,64,1024]{4,3,2,1,0:T(8,128)(2,1)}) custom-call(bf16[64,1664]{1,0:T(8,128)(2,1)} %pad.15.refs_0_, bf16[64,1024]{1,0:T(8,128)(2,1)} %pad.16.refs_1_), custom_call_target="tpu_custom_call" | custom-call | tf_op jit(solution)/shard_map/pallas_call | solution.py:177
  43.7 3.2 fusion.111
  48.0 2.5 copy.38
  55.9 33.9 %shard_map.195 = bf16[8,256,640]{2,1,0:T(8,128)(2,1)} custom-call(bf16[256,640]{1,0:T(8,128)(2,1)} %pad_maximum_fusion.6.block), custom_call_target="tpu_custom_call" | custom-call | tf_op jit(solution)/shard_map/pallas_call | solution.py:376
  89.8 4.9 copy.41
  94.7 5.3 reshape_reshape.6
  100.0 3.0 slice_bitcast_fusion
  103.0 35.6 %while.28 = (s32[]{:T(128)}, bf16[5,3,256,64]{2,3,1,0:T(8,128)(2,1)}, f32[5,3,256,1]{2,1,3,0:T(4,128)S(1)}, bf16[5,3,256,64]{2,3,1,0:T(8,128)(2,1)S(1)}, bf16[5,...) while((s32[]{:T(128)}, ...), condition=%wide.region_4.5_spmd.clone, body=%wide.region_1.4_spmd.clone.sunk | while | flops 420527616 | bytes 21725284 | solution.py:552
  104.8 1.9 exponential_reduce_fusion.2
  106.7 3.4 fusion.163
  111.8 1.9 exponential_reduce_fusion.2
  113.7 3.4 fusion.163
  118.9 1.9 exponential_reduce_fusion.2
  120.7 3.4 fusion.163
  125.9 1.9 exponential_reduce_fusion.2
  127.8 3.4 fusion.163
  132.9 1.9 exponential_reduce_fusion.2
  134.8 3.4 fusion.163
  138.7 2.1 fusion.79
  146.2 81.3 %shard_map.196 = (bf16[2,4,2,64,2560]{4,3,2,1,0:T(8,128)(2,1)}, bf16[2,4,2,64,2560]{4,3,2,1,0:T(8,128)(2,1)}, bf16[2,4,2,160,1024]{4,3,2,1,0:T(8,128)(2,1)}) custom-call(bf16[64,2560]{1,0:T(8,128)(2,1)} %pad.17.refs_0_, bf16[64,2560]{1,0:T(8,128)(2,1)} %pad.18.refs_1_, bf16[160,1024]{1,0:T(8,128)(2,1)} %fusion.87.refs_2_), custom_call_target="tpu_custom_call" | custom-call | tf_op jit(solution)/shard_map/pallas_call | solution.py:177
  227.6 4.2 fusion.114
  234.9 4.5 multiply_convert_fusion.1
  239.4 7.0 %fusion.85 = bf16[1,256,960]{1,2,0:T(8,128)(2,1)} fusion(s32[960]{0:T(1024)S(1)} %fusion.107, f32[256,1024]{0,1:T(8,128)} %copy-done.4, bf16[256,2560]{1,0:T(8,128)(2,1)} %get-tuple-element.216, bf16[2560,1024]{1,0:T(8,128)(2,1)} %bitcast.250), kind=kOutput, calls=%fused_computation.113 | convolution fusion | flops 1847246848 | bytes 8097536 | tf_op jit(solution)/shard_map/dot_general | solution.py:455
  246.4 4.6 fusion.116
  253.3 4.2 fusion.82
  257.5 63.0 %while.29 = (s32[]{:T(128)}, f32[5,3,256,64]{2,3,1,0:T(8,128)}, bf16[5,2048,64]{1,2,0:T(8,128)(2,1)}, bf16[5,2048,64]{1,2,0:T(8,128)(2,1)}, bf16[5,3,256,64]{2,3...) while((s32[]{:T(128)}, f32[5,3,256,64]{2,3,1,0:T(8,128)}, ...), condition=%wide.region_9.10_spmd.clone, body=%wide.region_7.9_spmd.clone.sunk | while | flops 1021492736 | bytes 50683004 | solution.py:597
  257.5 2.0 fusion.172
  259.9 3.2 multiply_reduce_fusion.8
  265.5 2.3 fusion.174
  267.7 2.3 fusion.175
  270.0 2.0 fusion.172
  272.4 3.2 multiply_reduce_fusion.8
  276.3 1.8 fusion.173
  278.0 2.3 fusion.174
  280.3 2.3 fusion.175
  282.6 2.0 fusion.172
  285.0 3.2 multiply_reduce_fusion.8
  290.6 2.3 fusion.174
  292.9 2.3 fusion.175
  295.1 2.0 fusion.172
  297.5 3.2 multiply_reduce_fusion.8
  303.1 2.3 fusion.174
  305.4 2.3 fusion.175
  307.7 2.0 fusion.172
  310.1 3.2 multiply_reduce_fusion.8
  315.7 2.3 fusion.174
  317.9 2.3 fusion.175
  320.4 2.0 pad_maximum_fusion
  322.4 2.4 copy.58
  324.8 4.8 copy.45.parts
  329.6 36.3 %shard_map.197 = f32[256,640]{1,0:T(8,128)} custom-call(bf16[8,256,640]{2,1,0:T(8,128)(2,1)} %copy.45.parts), custom_call_target="tpu_custom_call" | custom-call | tf_op jit(solution)/shard_map/pallas_call | solution.py:415
  371.6 1.8 fusion.84
  373.4 2.8 convolution_convert_fusion.3
  376.2 5.4 copy.49
  382.6 6.5 %concatenate.47.refs_0_ = bf16[2,4,2,64,1664]{4,3,2,1,0:T(8,128)(2,1)} concatenate(bf16[2,4,2,64,1600]{4,3,2,1,0:T(8,128)(2,1)} %bitcast.218, bf16[2,4,2,64,1]{4,3,2,1,0:T(8,128)(2,1)S(1)} %concatenate.48, bf16[2,4,2,64,1]{4,3,2,1,0:T(8,128)(2,1)S(1)} %concatenate.49, bf16[2,4,2,64,62]{4,3,2,1,0:T(8,128)(2,1)S(1)} %broadcast_in_dim.81), dimensions={4} | concatenate | bytes 6815744 | tf_op jit(solution)/shard_map/concatenate | solution.py:611
  389.2 2.1 convolution_convert_fusion.4
  391.3 48.4 %shard_map.198 = (bf16[64,1664]{1,0:T(8,128)(2,1)}, bf16[64,1024]{1,0:T(8,128)(2,1)}) custom-call(bf16[2,4,2,64,1664]{4,3,2,1,0:T(8,128)(2,1)} %concatenate.47.refs_0_, bf16[2,4,2,64,1024]{4,3,2,1,0:T(8,128)(2,1)} %bitcast.222), custom_call_target="tpu_custom_call" | custom-call | tf_op jit(solution)/shard_map/pallas_call | solution.py:343
  442.9 2.5 fusion.55
  445.4 3.8 convolution_convert_fusion.2
  449.3 3.9 convolution_convert_fusion.1
  453.2 3.9 convolution_convert_fusion
  457.1 97.6 %shard_map.199 = (bf16[64,2560]{1,0:T(8,128)(2,1)}, bf16[64,2560]{1,0:T(8,128)(2,1)}, bf16[160,1024]{1,0:T(8,128)(2,1)}) custom-call(bf16[2,4,2,64,2560]{4,3,2,1,0:T(8,128)(2,1)} %bitcast.207, bf16[2,4,2,64,2560]{4,3,2,1,0:T(8,128)(2,1)} %bitcast.208, bf16[2,4,2,160,1024]{4,3,2,1,0:T(8,128)(2,1)} %bitcast.209), custom_call_target="tpu_custom_call" | custom-call | tf_op jit(solution)/shard_map/pallas_call | solution.py:343
  554.7 2.3 slice_convert_fusion.2
  556.9 2.8 fusion.54
  (193 shorter events, 54.3 us)
Async XLA Ops:
  0.6 1.1 copy-start
  0.7 2.8 copy-start.28
  0.7 2.8 copy-start.29
  0.7 2.8 copy-start.30
  0.7 2.5 copy-start.33
  0.7 2.6 copy-start.34
  0.7 3.6 copy-start.37
  3.2 137.7 %copy-start.2 = (f32[256,1024]{0,1:T(8,128)}, f32[256,1024]{0,1:T(8,128)S(1)}, u32[]{:S(2)}) copy-start(f32[256,1024]{0,1:T(8,128)S(1)} %get-tuple-element.235) | copy-start | bytes 3145732
  43.1 0.6 copy-start.26
  43.7 4.3 copy-start.31
  51.3 4.6 copy-start.21
  138.6 3.2 copy-start.6
  138.7 2.2 copy-start.13
  140.8 2.2 copy-start.11
  140.8 2.2 copy-start.23
  140.8 3.0 copy-start.24
  140.8 3.7 copy-start.36
  141.8 1.0 copy-start.4
  227.6 4.2 slice-start
  227.6 4.2 slice-start.1
  227.6 7.3 %slice-start.4 = ((s8[5242880]{0:T(1024)(128)(4,1)}), s8[4194304]{0:T(1024)(128)(4,1)S(1)}, s32[]{:S(2)}) async-start(s8[5242880]{0:T(1024)(128)(4,1)} %bitcast.251), calls=%async_computation.4 | async-start | bytes 8388608
  231.8 1.6 copy-start.35
  231.8 3.1 slice-start.5
  234.9 4.5 copy-start.14
  239.4 11.6 %slice-start.2 = ((s8[5242880]{0:T(1024)(128)(4,1)}), s8[1048576]{0:T(1024)(128)(4,1)S(1)}, s32[]{:S(2)}) async-start(s8[5242880]{0:T(1024)(128)(4,1)} %bitcast.213), calls=%async_computation.2 | async-start | bytes 2097152
  246.4 4.6 slice-start.3
  246.4 4.6 copy-start.5
  246.4 4.8 copy-start.17
  251.2 1.7 copy-start.15
  253.2 4.2 copy-start.7
  329.6 38.9 %copy-start.22 = (f32[256,32]{0,1:T(8,128)S(1)}, f32[256,32]{0,1:T(8,128)}, u32[]{:S(2)}) copy-start(f32[256,32]{0,1:T(8,128)} %copy-done.21) | copy-start | bytes 98308
  329.6 38.9 %copy-start.25 = (f32[256,32]{0,1:T(8,128)S(1)}, f32[256,32]{0,1:T(8,128)}, u32[]{:S(2)}) copy-start(f32[256,32]{0,1:T(8,128)} %get-tuple-element.231) | copy-start | bytes 98308
  329.6 39.0 %copy-start.20 = (f32[5,3,256,64]{2,3,1,0:T(8,128)S(1)}, f32[5,3,256,64]{2,3,1,0:T(8,128)}, u32[]{:S(2)}) copy-start(f32[5,3,256,64]{2,3,1,0:T(8,128)} %get-tuple-element.120) | copy-start | bytes 2949124
  365.9 2.9 copy-start.3
  365.9 2.9 copy-start.27
  365.9 2.9 copy-start.32
  368.4 2.0 copy-start.9
  370.4 1.2 copy-start.8
  382.6 6.6 %copy-start.12 = (bf16[256,1024]{1,0:T(8,128)(2,1)S(1)}, bf16[256,1024]{1,0:T(8,128)(2,1)}, u32[]{:S(2)}) copy-start(bf16[256,1024]{1,0:T(8,128)(2,1)} %copy-done.11) | copy-start | bytes 1572868
  391.3 54.1 %copy-start.19 = (bf16[256,2560]{1,0:T(8,128)(2,1)S(1)}, bf16[256,2560]{1,0:T(8,128)(2,1)}, u32[]{:S(2)}) copy-start(bf16[256,2560]{1,0:T(8,128)(2,1)} %get-tuple-element.215) | copy-start | bytes 3932164
  445.4 3.8 copy-start.18
  449.2 3.9 copy-start.10
  449.2 3.9 copy-start.16
  457.1 102.7 %copy-start.1 = (bf16[1,256,960]{1,2,0:T(8,128)(2,1)S(1)}, bf16[1,256,960]{1,2,0:T(8,128)(2,1)}, u32[]{:S(2)}) copy-start(bf16[1,256,960]{1,2,0:T(8,128)(2,1)} %param.15) | copy-start | bytes 1474564
